TPU v7x, 256 devices: a whole 4x4x8 slice. The times are simulated.
256 devices in a mesh: dp: 8 (over y, core), expert: 32 (over z, x).
Axes of the slice: x: 4, y: 4, z: 8, core: 2. Of those that a mesh axis runs over, the one named last changes fastest.
Arguments:
- tokens: bfloat16 [12288, 2048], P(('dp', 'expert')), may hold values from -6 to 6
- expert_ids: int32 [12288, 8], P(('dp', 'expert')), may hold values from 0 to 31, all different within a row; in each aligned block of 48 rows (0 to 47, 48 to 95, ...) at most 18 rows name the same one
- gate_weights: float32 [12288, 8], P(('dp', 'expert')), may hold values from 0.05 to 1
- up_weight: bfloat16 [32, 2048, 768], P('expert'), may hold values from -0.125 to 0.125
- down_weight: bfloat16 [32, 768, 2048], P('expert'), may hold values from -0.21875 to 0.21875
- out_grad: bfloat16 [12288, 2048], P(('dp', 'expert')), may hold values from -0.59765625 to 0.59765625
Outputs:
- mixed: bfloat16 [12288, 2048], P(('dp', 'expert'))
- grad_tokens: bfloat16 [12288, 2048], P(('dp', 'expert'))
- grad_up: bfloat16 [32, 2048, 768], P('expert')
- grad_down: bfloat16 [32, 768, 2048], P('expert')
Inputs may be any that keep to these rules, and one draw needn't show every extreme that they name: `expert_ids`: the 8 experts of a token are distinct. Among the 48 tokens of one device at most 18 name any one expert, and in every draw some device has 18 tokens naming one expert.
All inputs are finite; a program needn't handle non-finite values.
Results may differ from a plain program's by a relative error of at most 0.017.
Values may be sent and summed in bfloat16 or wider, within the bound.
A program may use at most 128 MiB of HBM per device.

v0:
```python
import jax
import jax.numpy as jnp
from jax import lax
from jax.sharding import PartitionSpec as P


def silu_slope(pre_act):
    sigmoid = jax.nn.sigmoid(pre_act)
    return sigmoid * (1.0 + pre_act * (1.0 - sigmoid))


def contract(left, right, left_dim, right_dim):
    return lax.dot_general(
        left, right, (((left_dim,), (right_dim,)), ((), ())), preferred_element_type=jnp.float32
    )


def forward_block(rows_x, up_local, down_local):
    pre_act = jnp.dot(rows_x, up_local, preferred_element_type=jnp.float32)
    hidden = jax.nn.silu(pre_act).astype(jnp.bfloat16)
    expert_out = jnp.dot(hidden, down_local, preferred_element_type=jnp.float32).astype(
        jnp.bfloat16
    )
    return (pre_act, hidden, expert_out)


def backward_block(rows_dy, pre_act, up_local, down_local):
    linear = contract(rows_dy, down_local, 1, 1)
    pre_grad = (linear * silu_slope(pre_act)).astype(jnp.bfloat16)
    grad_rows = contract(pre_grad, up_local, 1, 1).astype(jnp.bfloat16)
    return (pre_grad, grad_rows)


def shards(tokens, expert_ids, gate_weights, up_weight, down_weight, out_grad):
    experts = lax.axis_size("expert")
    tok_count, top_count = expert_ids.shape
    slot_rows = tok_count * top_count * 3 // (2 * experts)
    recv_rows = experts * slot_rows
    model_width = tokens.shape[1]
    up_local = up_weight[0]
    down_local = down_weight[0]
    matches = (
        expert_ids[:, :, None] == jnp.arange(experts, dtype=jnp.int32)[None, None, :]
    ).astype(jnp.int32)
    hit_table = jnp.sum(matches, axis=1)
    before = jnp.cumsum(hit_table, axis=0) - hit_table
    slot_place = jnp.sum(matches * before[:, None, :], axis=2)
    target = (expert_ids * slot_rows + slot_place).reshape(-1)
    source = jnp.repeat(
        jnp.arange(tok_count, dtype=jnp.int32), top_count, total_repeat_length=tok_count * top_count
    )
    counts = jnp.sum(hit_table, axis=0).astype(jnp.bfloat16).reshape(experts, 1)
    send_x = jnp.zeros((recv_rows, model_width), jnp.bfloat16).at[target].set(tokens[source])
    send_x = send_x.reshape(experts, slot_rows, model_width)
    scaled = (gate_weights.reshape(-1)[:, None] * out_grad[source].astype(jnp.float32)).astype(
        jnp.bfloat16
    )
    send_dy = jnp.zeros((recv_rows, model_width), jnp.bfloat16).at[target].set(scaled)
    send_dy = send_dy.reshape(experts, slot_rows, model_width)
    got_x, got_counts = (
        lax.all_to_all(send_x, "expert", split_axis=0, concat_axis=0, tiled=True),
        lax.all_to_all(counts, "expert", split_axis=0, concat_axis=0, tiled=True),
    )
    x_rows = got_x.reshape(recv_rows, model_width)
    pre_rows, hidden_rows, out_rows = forward_block(x_rows, up_local, down_local)
    back_out = lax.all_to_all(
        out_rows.reshape(experts, slot_rows, model_width),
        "expert",
        split_axis=0,
        concat_axis=0,
        tiled=True,
    )
    gathered = back_out.reshape(recv_rows, model_width)[target].reshape(
        tok_count, top_count, model_width
    )
    mixed = jnp.sum(gate_weights[:, :, None] * gathered.astype(jnp.float32), axis=1).astype(
        jnp.bfloat16
    )
    got_dy = lax.all_to_all(send_dy, "expert", split_axis=0, concat_axis=0, tiled=True)
    dy_rows = got_dy.reshape(recv_rows, model_width)
    down_grad = contract(hidden_rows, dy_rows, 0, 0)
    pre_grad, grad_rows = backward_block(dy_rows, pre_rows, up_local, down_local)
    up_grad = contract(x_rows, pre_grad, 0, 0)
    back_grad = lax.all_to_all(
        grad_rows.reshape(experts, slot_rows, model_width),
        "expert",
        split_axis=0,
        concat_axis=0,
        tiled=True,
    )
    grad_pairs = back_grad.reshape(recv_rows, model_width)[target].reshape(
        tok_count, top_count, model_width
    )
    grad_tokens = jnp.sum(grad_pairs.astype(jnp.float32), axis=1).astype(jnp.bfloat16)
    up_sum, down_sum = (
        lax.psum(up_grad.astype(jnp.bfloat16), "dp").astype(jnp.float32),
        lax.psum(down_grad.astype(jnp.bfloat16), "dp").astype(jnp.float32),
    )
    return (
        mixed,
        grad_tokens,
        up_sum.astype(jnp.bfloat16)[None],
        down_sum.astype(jnp.bfloat16)[None],
    )


def solution(mesh):
    return jax.shard_map(
        shards,
        mesh=mesh,
        in_specs=(
            P(("dp", "expert"), None),
            P(("dp", "expert"), None),
            P(("dp", "expert"), None),
            P("expert", None, None),
            P("expert", None, None),
            P(("dp", "expert"), None),
        ),
        out_specs=(
            P(("dp", "expert"), None),
            P(("dp", "expert"), None),
            P("expert", None, None),
            P("expert", None, None),
        ),
        check_vma=False,
    )
```

profile of v0, /device:TPU:1, one launch (start us, length us, event | category | flops | bytes accessed | tf_op | source)
XLA Modules:
  0.0 419.1 jit_solution(2827004243275815858)
XLA Ops:
  10.9 4.5 %fusion.27 = (s32[384]{0:T(512)S(1)}, s32[384,1]{0,1:T(1,128)S(1)}) fusion(s32[]{:T(128)} %bitcast.41, s32[]{:T(128)} %bitcast.42, s32[]{:T(128)} %bitcast.43, s32[]{:T(128)} %bitcast.44, s32[]{:T(128)} %bitcast.45, s32[]{:T(128)} %bitcast.47, s32[]{:T(128)} %bitcast.46, s32[1,1,3,128]{3,2,1,0:T(4,128)S(1)} %get-tuple-element.62, ...), kind=kLoop, calls=%fused_computation.95 | loop fusion | flops 5376 | bytes 6172 | tf_op jit(solution)/shard_map/jit(_take)/gather | solution.py:49
  15.6 25.6 %select_select_fusion = s32[384]{0:T(512)S(1)} fusion(pred[384]{0:T(512)(128)(4,1)S(1)} %get-tuple-element.55, pred[384]{0:T(512)(128)(4,1)S(1)} %get-tuple-element.54, pred[384]{0:T(512)(128)(4,1)S(1)} %get-tuple-element.56, pred[384]{0:T(512)(128)(4,1)S(1)} %get-tuple-element.53, pred[384]{0:T(512)(128)(4,1)S(1)} %get-tuple-element.52, ...), kind=kLoop, calls=%fused_computation.94 | loop fusion | flops 15744 | bytes 18980 | tf_op jit(solution)/shard_map/jit(_take)/gather | solution.py:49
  43.0 10.9 %scatter_custom_fusion = bf16[576,2048]{1,0:T(8,128)(2,1)} fusion(s32[384]{0:T(512)S(1)} %fusion.28, bf16[48,2048]{1,0:T(8,128)(2,1)} %param.8, s32[1024]{0:T(1024)S(1)} %pad_clamp_fusion.1, bf16[]{:T(256)} %constant.95.clone.1), kind=kCustom, calls=%fused_computation.28 | custom fusion | bytes 2359808 | tf_op jit(solution)/shard_map/scatter | solution.py:53
  53.9 4.3 %reshape.186 = bf16[32,18,2048]{2,1,0:T(8,128)(2,1)} reshape(bf16[576,2048]{1,0:T(8,128)(2,1)} %scatter_custom_fusion) | data formatting | bytes 4718592 | tf_op jit(solution)/shard_map/reshape | solution.py:54
  58.2 12.3 %all-to-all-start = ((bf16[32,18,2048]{2,1,0:T(8,128)(2,1)}), bf16[32,18,2048]{2,1,0:T(8,128)(2,1)}, u32[]{:S(2)}, u32[]{:S(2)}) async-start(bf16[32,18,2048]{2,1,0:T(8,128)(2,1)} %reshape.186), calls=%async_computation | async-start | bytes 6291456 | tf_op jit(solution)/shard_map/all_to_all | solution.py:61
  70.7 9.6 %scatter_custom_fusion.1 = bf16[576,2048]{1,0:T(8,128)(2,1)} fusion(s32[384]{0:T(512)S(1)} %fusion.28, f32[384]{0:T(512)S(1)} %mul.52, bf16[]{:T(256)} %constant.95.clone.1, bf16[48,2048]{1,0:T(8,128)(2,1)S(1)} %copy-done.6, s32[1024]{0:T(1024)S(1)} %pad_clamp_fusion.1), kind=kCustom, calls=%fused_computation.26 | custom fusion | flops 2359296 | bytes 2562050 | tf_op jit(solution)/shard_map/scatter | solution.py:58
  80.3 4.3 %reshape.190 = bf16[32,18,2048]{2,1,0:T(8,128)(2,1)} reshape(bf16[576,2048]{1,0:T(8,128)(2,1)} %scatter_custom_fusion.1) | data formatting | bytes 4718592 | tf_op jit(solution)/shard_map/reshape | solution.py:59
  84.6 56.4 %all-to-all-done = bf16[32,18,2048]{2,1,0:T(8,128)(2,1)} async-done(((bf16[32,18,2048]{2,1,0:T(8,128)(2,1)}), bf16[32,18,2048]{2,1,0:T(8,128)(2,1)}, u32[]{:S(2)}, u32[]{:S(2)}) %all-to-all-start) | async-done | bytes 2359328 | tf_op jit(solution)/shard_map/all_to_all | solution.py:61
  141.0 7.9 %all-to-all-start.2 = ((bf16[32,18,2048]{2,1,0:T(8,128)(2,1)}), bf16[32,18,2048]{2,1,0:T(8,128)(2,1)}, u32[]{:S(2)}, u32[]{:S(2)}) async-start(bf16[32,18,2048]{2,1,0:T(8,128)(2,1)} %reshape.190), calls=%async_computation.2 | async-start | bytes 6291456 | tf_op jit(solution)/shard_map/all_to_all | solution.py:79
  148.9 4.4 %reshape.187 = bf16[576,2048]{1,0:T(8,128)(2,1)} reshape(bf16[32,18,2048]{2,1,0:T(8,128)(2,1)} %all-to-all-done) | data formatting | bytes 4718592 | tf_op jit(solution)/shard_map/reshape | solution.py:64
  153.3 4.6 %fusion.7 = f32[576,768]{1,0:T(8,128)S(1)} fusion(bf16[576,2048]{1,0:T(8,128)(2,1)} %reshape.187, bf16[1,2048,768]{2,1,0:T(8,128)(2,1)} %param.11), kind=kOutput, calls=%fused_computation.16 | convolution fusion | flops 1811939328 | bytes 7274496 | tf_op jit(solution)/shard_map/dot_general | solution.py:19
  159.1 3.5 fusion.12
  162.5 4.3 %reshape.188 = bf16[32,18,2048]{2,1,0:T(8,128)(2,1)} reshape(bf16[576,2048]{1,0:T(8,128)(2,1)} %fusion.12) | data formatting | bytes 4718592 | tf_op jit(solution)/shard_map/reshape | solution.py:67
  166.8 52.9 %all-to-all-done.2 = bf16[32,18,2048]{2,1,0:T(8,128)(2,1)} async-done(((bf16[32,18,2048]{2,1,0:T(8,128)(2,1)}), bf16[32,18,2048]{2,1,0:T(8,128)(2,1)}, u32[]{:S(2)}, u32[]{:S(2)}) %all-to-all-start.2) | async-done | bytes 2359328 | tf_op jit(solution)/shard_map/all_to_all | solution.py:79
  219.7 6.6 %all-to-all-start.1 = ((bf16[32,18,2048]{2,1,0:T(8,128)(2,1)}), bf16[32,18,2048]{2,1,0:T(8,128)(2,1)}, u32[]{:S(2)}, u32[]{:S(2)}) async-start(bf16[32,18,2048]{2,1,0:T(8,128)(2,1)} %reshape.188), calls=%async_computation.1 | async-start | bytes 6291456 | tf_op jit(solution)/shard_map/all_to_all | solution.py:66
  226.4 4.4 %reshape.191 = bf16[576,2048]{1,0:T(8,128)(2,1)} reshape(bf16[32,18,2048]{2,1,0:T(8,128)(2,1)} %all-to-all-done.2) | data formatting | bytes 4718592 | tf_op jit(solution)/shard_map/reshape | solution.py:80
  230.8 4.6 %multiply_convert_fusion.1 = bf16[576,768]{1,0:T(8,128)(2,1)S(1)} fusion(f32[576,768]{1,0:T(8,128)} %copy-done.9, bf16[576,2048]{1,0:T(8,128)(2,1)} %reshape.191, bf16[1,768,2048]{2,1,0:T(8,128)(2,1)S(1)} %copy-done), kind=kOutput, calls=%fused_computation.23 | convolution fusion | flops 1815920640 | bytes 8159232 | tf_op jit(solution)/shard_map/dot_general | solution.py:13
  240.8 55.6 %all-to-all-done.1 = bf16[32,18,2048]{2,1,0:T(8,128)(2,1)} async-done(((bf16[32,18,2048]{2,1,0:T(8,128)(2,1)}), bf16[32,18,2048]{2,1,0:T(8,128)(2,1)}, u32[]{:S(2)}, u32[]{:S(2)}) %all-to-all-start.1) | async-done | bytes 2359328 | tf_op jit(solution)/shard_map/all_to_all | solution.py:66
  296.4 6.8 %all-to-all-start.3 = ((bf16[32,18,2048]{2,1,0:T(8,128)(2,1)}), bf16[32,18,2048]{2,1,0:T(8,128)(2,1)}, u32[]{:S(2)}, u32[]{:S(2)}) async-start(bf16[32,18,2048]{2,1,0:T(8,128)(2,1)} %reshape.192), calls=%async_computation.3 | async-start | bytes 6291456 | tf_op jit(solution)/shard_map/all_to_all | solution.py:84
  303.5 5.4 %fusion.15 = bf16[1,2048,768]{2,1,0:T(8,128)(2,1)} fusion(bf16[576,2048]{1,0:T(8,128)(2,1)S(1)} %copy-done.4, bf16[576,768]{1,0:T(8,128)(2,1)} %copy-done.11), kind=kOutput, calls=%fused_computation.21 | convolution fusion | flops 1813512192 | bytes 6389760 | tf_op jit(solution)/shard_map/dot_general | solution.py:13
  308.9 4.1 fusion.16
  319.1 53.4 %all-to-all-done.3 = bf16[32,18,2048]{2,1,0:T(8,128)(2,1)} async-done(((bf16[32,18,2048]{2,1,0:T(8,128)(2,1)}), bf16[32,18,2048]{2,1,0:T(8,128)(2,1)}, u32[]{:S(2)}, u32[]{:S(2)}) %all-to-all-start.3) | async-done | bytes 2359328 | tf_op jit(solution)/shard_map/all_to_all | solution.py:84
  384.1 22.6 %all-reduce.3.cloned.1.call-done = (bf16[1,2048,768]{2,1,0:T(8,128)(2,1)}, bf16[1,768,2048]{2,1,0:T(8,128)(2,1)}) async-done(((bf16[1,2048,768]{2,1,0:T(8,128)(2,1)}, bf16[1,768,2048]{2,1,0:T(8,128)(2,1)}), (bf16[1,2048,768]{2,1,0:T(8,128)(2,1)}, bf16[1,768,2048]{2,1,0:T(8,128)(2,1)})) %all-reduce.3.cloned.1.call-update) | async-done | bytes 6291472 | tf_op jit(solution)/shard_map/psum | solution.py:96
  406.7 3.9 copy.30
  (57 shorter events, 32.2 us)
Async XLA Ops:
  7.2 151.9 %copy-start = (bf16[1,768,2048]{2,1,0:T(8,128)(2,1)S(1)}, bf16[1,768,2048]{2,1,0:T(8,128)(2,1)}, u32[]{:S(2)}) copy-start(bf16[1,768,2048]{2,1,0:T(8,128)(2,1)} %param.12) | copy-start | bytes 9437188
  58.2 12.3 %copy-start.7 = (f32[48,8]{0,1:T(8,128)S(1)}, f32[48,8]{0,1:T(8,128)}, u32[]{:S(2)}) copy-start(f32[48,8]{0,1:T(8,128)} %param.10) | copy-start | bytes 4612
  58.2 12.5 %copy-start.6 = (bf16[48,2048]{1,0:T(8,128)(2,1)S(1)}, bf16[48,2048]{1,0:T(8,128)(2,1)}, u32[]{:S(2)}) copy-start(bf16[48,2048]{1,0:T(8,128)(2,1)} %param.13) | copy-start | bytes 589828
  58.2 82.8 %all-to-all-start = ((bf16[32,18,2048]{2,1,0:T(8,128)(2,1)}), bf16[32,18,2048]{2,1,0:T(8,128)(2,1)}, u32[]{:S(2)}, u32[]{:S(2)}) async-start(bf16[32,18,2048]{2,1,0:T(8,128)(2,1)} %reshape.186), calls=%async_computation | async-start | bytes 6291456 | tf_op jit(solution)/shard_map/all_to_all | solution.py:61
  141.0 78.7 %all-to-all-start.2 = ((bf16[32,18,2048]{2,1,0:T(8,128)(2,1)}), bf16[32,18,2048]{2,1,0:T(8,128)(2,1)}, u32[]{:S(2)}, u32[]{:S(2)}) async-start(bf16[32,18,2048]{2,1,0:T(8,128)(2,1)} %reshape.190), calls=%async_computation.2 | async-start | bytes 6291456 | tf_op jit(solution)/shard_map/all_to_all | solution.py:79
  157.9 1.2 copy-start.9
  219.7 76.7 %all-to-all-start.1 = ((bf16[32,18,2048]{2,1,0:T(8,128)(2,1)}), bf16[32,18,2048]{2,1,0:T(8,128)(2,1)}, u32[]{:S(2)}, u32[]{:S(2)}) async-start(bf16[32,18,2048]{2,1,0:T(8,128)(2,1)} %reshape.188), calls=%async_computation.1 | async-start | bytes 6291456 | tf_op jit(solution)/shard_map/all_to_all | solution.py:66
  230.8 5.6 %copy-start.8 = (bf16[1,2048,768]{2,1,0:T(8,128)(2,1)S(1)}, bf16[1,2048,768]{2,1,0:T(8,128)(2,1)}, u32[]{:S(2)}) copy-start(bf16[1,2048,768]{2,1,0:T(8,128)(2,1)} %param.11) | copy-start | bytes 9437188
  235.4 1.0 copy-start.11
  240.8 62.7 %copy-start.4 = (bf16[576,2048]{1,0:T(8,128)(2,1)S(1)}, bf16[576,2048]{1,0:T(8,128)(2,1)}, u32[]{:S(2)}) copy-start(bf16[576,2048]{1,0:T(8,128)(2,1)} %reshape.187) | copy-start | bytes 7077892
  296.4 76.1 %all-to-all-start.3 = ((bf16[32,18,2048]{2,1,0:T(8,128)(2,1)}), bf16[32,18,2048]{2,1,0:T(8,128)(2,1)}, u32[]{:S(2)}, u32[]{:S(2)}) async-start(bf16[32,18,2048]{2,1,0:T(8,128)(2,1)} %reshape.192), calls=%async_computation.3 | async-start | bytes 6291456 | tf_op jit(solution)/shard_map/all_to_all | solution.py:84
  303.2 103.5 %all-reduce.3.cloned.1.call-start = ((), (), s32[]{:S(2)}) async-start(), calls=%async_computation.4 | async-start | bytes 12582912 | tf_op jit(solution)/shard_map/psum | solution.py:96
  303.5 5.4 %copy-start.5 = (bf16[576,2048]{1,0:T(8,128)(2,1)S(1)}, bf16[576,2048]{1,0:T(8,128)(2,1)}, u32[]{:S(2)}) copy-start(bf16[576,2048]{1,0:T(8,128)(2,1)} %reshape.191) | copy-start | bytes 7077892
  303.5 5.4 %copy-start.10 = (f32[576,768]{1,0:T(8,128)S(1)}, f32[576,768]{1,0:T(8,128)}, u32[]{:S(2)}) copy-start(f32[576,768]{1,0:T(8,128)} %copy-done.9) | copy-start | bytes 5308420
  378.7 3.3 copy-start.2
  406.7 3.9 copy-start.3
  406.7 5.6 %copy-start.1 = (bf16[1,768,2048]{2,1,0:T(8,128)(2,1)S(1)}, bf16[1,768,2048]{2,1,0:T(8,128)(2,1)}, u32[]{:S(2)}) copy-start(bf16[1,768,2048]{2,1,0:T(8,128)(2,1)} %param.12) | copy-start | bytes 9437188
Sparse Core Ops, SparseCore 0:
  313.1 93.5 all-reduce.2
where the time goes:
time: 421 us; the launch traced here: 419 us
  waiting for transfers between devices  241 us (57%)
  local copies, waits for them, and re-layouts  57.6 us (14%)
  other arithmetic  48.4 us (11%)
  starting transfers between devices  33.9 us (8%)
  matrix products  24.1 us (6%)
  between operations  14.2 us (3%)
    all_to_all x1, waiting for transfers between devices, shards(): lax.all_to_all(send_x, 'expert', split_axis=0, concat_axis=0, tiled=True)  56.4 us
    all_to_all x1, waiting for transfers between devices, shards(): lax.all_to_all(out_rows.reshape(experts, slot_rows, model_width), 'expert...  55.6 us
    all_to_all x1, waiting for transfers between devices, shards(): lax.all_to_all(grad_rows.reshape(experts, slot_rows, model_width), 'exper...  53.4 us
    all_to_all x1, waiting for transfers between devices, shards(): lax.all_to_all(send_dy, 'expert', split_axis=0, concat_axis=0, tiled=True)  52.9 us
    gather x3, other arithmetic, shards(): jnp.repeat(jnp.arange(tok_count, dtype=jnp.int32), top_count, total_repea...  30.3 us
    psum x1, waiting for transfers between devices, shards(): lax.psum(up_grad.astype(jnp.bfloat16), 'dp').astype(jnp.float32)  22.6 us
    dot_general x4, matrix products, contract(): lax.dot_general(left, right, (((left_dim,), (right_dim,)), ((), ())), pre...  16.1 us
    all_to_all x1, starting transfers between devices, shards(): lax.all_to_all(send_x, 'expert', split_axis=0, concat_axis=0, tiled=True)  12.3 us
  transfers between devices with their start and end apart: 5, of which 5 were waited for; matrix products, arithmetic and copies ran while one was open for 17% of the time, Pallas kernels for 0%

commit v1 on v0

--- a/solution.py
+++ b/solution.py
@@ -93,7 +93,7 @@
     )
     grad_tokens = jnp.sum(grad_pairs.astype(jnp.float32), axis=1).astype(jnp.bfloat16)
     up_sum, down_sum = (
-        lax.psum(up_grad.astype(jnp.bfloat16), "dp").astype(jnp.float32),
+        jnp.sum(lax.all_gather(up_grad.astype(jnp.bfloat16), "dp"), axis=0).astype(jnp.float32),
         lax.psum(down_grad.astype(jnp.bfloat16), "dp").astype(jnp.float32),
     )
     return (

time: 421 us -> 453 us (1.076)
  the two profiles are of different devices: /device:TPU:1 before, /device:TPU:2 now
where the time goes in v1:
time: 453 us; the launch traced here: 445 us
  waiting for transfers between devices  243 us (54%)
  other arithmetic  64 us (14%)
  local copies, waits for them, and re-layouts  57.4 us (13%)
  starting transfers between devices  33.6 us (7%)
  matrix products  32.8 us (7%)
  between operations  14.4 us (3%)
    all_to_all x1, waiting for transfers between devices, shards(): lax.all_to_all(out_rows.reshape(experts, slot_rows, model_width), 'expert...  60.8 us
    all_to_all x1, waiting for transfers between devices, shards(): lax.all_to_all(send_dy, 'expert', split_axis=0, concat_axis=0, tiled=True)  60.3 us
    all_to_all x1, waiting for transfers between devices, shards(): lax.all_to_all(grad_rows.reshape(experts, slot_rows, model_width), 'exper...  58.1 us
    all_to_all x1, waiting for transfers between devices, shards(): lax.all_to_all(send_x, 'expert', split_axis=0, concat_axis=0, tiled=True)  57 us
    gather x3, other arithmetic, shards(): jnp.repeat(jnp.arange(tok_count, dtype=jnp.int32), top_count, total_repea...  30.3 us
    dot_general x4, matrix products, contract(): lax.dot_general(left, right, (((left_dim,), (right_dim,)), ((), ())), pre...  22 us
    reduce_sum x1, other arithmetic, shards(): jnp.sum(lax.all_gather(up_grad.astype(jnp.bfloat16), 'dp'), axis=0)  15.6 us
    all_to_all x1, starting transfers between devices, shards(): lax.all_to_all(send_x, 'expert', split_axis=0, concat_axis=0, tiled=True)  12.4 us
  transfers between devices with their start and end apart: 6, of which 5 were waited for; matrix products, arithmetic and copies ran while one was open for 19% of the time, Pallas kernels for 0%

profile of v1, /device:TPU:2, one launch (start us, length us, event | category | flops | bytes accessed | tf_op | source)
XLA Modules:
  0.0 445.0 jit_solution(7503105343783433074)
XLA Ops:
  10.9 4.5 %fusion.26 = (s32[384]{0:T(512)S(1)}, s32[384,1]{0,1:T(1,128)S(1)}) fusion(s32[]{:T(128)} %bitcast.41, s32[]{:T(128)} %bitcast.42, s32[]{:T(128)} %bitcast.43, s32[]{:T(128)} %bitcast.44, s32[]{:T(128)} %bitcast.45, s32[]{:T(128)} %bitcast.47, s32[]{:T(128)} %bitcast.46, s32[1,1,3,128]{3,2,1,0:T(4,128)S(1)} %get-tuple-element.60, ...), kind=kLoop, calls=%fused_computation.94 | loop fusion | flops 5376 | bytes 6172 | tf_op jit(solution)/shard_map/jit(_take)/gather | solution.py:49
  15.6 25.6 %select_select_fusion = s32[384]{0:T(512)S(1)} fusion(pred[384]{0:T(512)(128)(4,1)S(1)} %get-tuple-element.55, pred[384]{0:T(512)(128)(4,1)S(1)} %get-tuple-element.54, pred[384]{0:T(512)(128)(4,1)S(1)} %get-tuple-element.56, pred[384]{0:T(512)(128)(4,1)S(1)} %get-tuple-element.53, pred[384]{0:T(512)(128)(4,1)S(1)} %get-tuple-element.52, ...), kind=kLoop, calls=%fused_computation.93 | loop fusion | flops 15744 | bytes 18980 | tf_op jit(solution)/shard_map/jit(_take)/gather | solution.py:49
  43.0 10.2 %scatter_custom_fusion = bf16[576,2048]{1,0:T(8,128)(2,1)} fusion(s32[384]{0:T(512)S(1)} %fusion.27, bf16[48,2048]{1,0:T(8,128)(2,1)} %param.8, s32[1024]{0:T(1024)S(1)} %pad_clamp_fusion.1, bf16[]{:T(256)} %constant.96.clone.1), kind=kCustom, calls=%fused_computation.27 | custom fusion | bytes 2359808 | tf_op jit(solution)/shard_map/scatter | solution.py:53
  53.2 4.3 reshape.186
  57.5 12.4 %all-to-all-start = ((bf16[32,18,2048]{2,1,0:T(8,128)(2,1)}), bf16[32,18,2048]{2,1,0:T(8,128)(2,1)}, u32[]{:S(2)}, u32[]{:S(2)}) async-start(bf16[32,18,2048]{2,1,0:T(8,128)(2,1)} %reshape.186), calls=%async_computation | async-start | bytes 6291456 | tf_op jit(solution)/shard_map/all_to_all | solution.py:61
  70.1 9.6 %scatter_custom_fusion.1 = bf16[576,2048]{1,0:T(8,128)(2,1)} fusion(s32[384]{0:T(512)S(1)} %fusion.27, f32[384]{0:T(512)S(1)} %mul.52, bf16[]{:T(256)} %constant.96.clone.1, bf16[48,2048]{1,0:T(8,128)(2,1)S(1)} %copy-done.5, s32[1024]{0:T(1024)S(1)} %pad_clamp_fusion.1), kind=kCustom, calls=%fused_computation.25 | custom fusion | flops 2359296 | bytes 2562050 | tf_op jit(solution)/shard_map/scatter | solution.py:58
  79.7 4.3 reshape.190
  84.0 57.0 %all-to-all-done = bf16[32,18,2048]{2,1,0:T(8,128)(2,1)} async-done(((bf16[32,18,2048]{2,1,0:T(8,128)(2,1)}), bf16[32,18,2048]{2,1,0:T(8,128)(2,1)}, u32[]{:S(2)}, u32[]{:S(2)}) %all-to-all-start) | async-done | bytes 2359328 | tf_op jit(solution)/shard_map/all_to_all | solution.py:61
  141.0 7.4 %all-to-all-start.2 = ((bf16[32,18,2048]{2,1,0:T(8,128)(2,1)}), bf16[32,18,2048]{2,1,0:T(8,128)(2,1)}, u32[]{:S(2)}, u32[]{:S(2)}) async-start(bf16[32,18,2048]{2,1,0:T(8,128)(2,1)} %reshape.190), calls=%async_computation.2 | async-start | bytes 6291456 | tf_op jit(solution)/shard_map/all_to_all | solution.py:79
  148.6 4.3 reshape.187
  153.0 5.8 %fusion.7 = f32[576,768]{1,0:T(8,128)} fusion(bf16[576,2048]{1,0:T(8,128)(2,1)} %reshape.187, bf16[1,2048,768]{2,1,0:T(8,128)(2,1)} %param.11), kind=kOutput, calls=%fused_computation.16 | convolution fusion | flops 1811939328 | bytes 7274496 | tf_op jit(solution)/shard_map/dot_general | solution.py:19
  158.8 60.3 %all-to-all-done.2 = bf16[32,18,2048]{2,1,0:T(8,128)(2,1)} async-done(((bf16[32,18,2048]{2,1,0:T(8,128)(2,1)}), bf16[32,18,2048]{2,1,0:T(8,128)(2,1)}, u32[]{:S(2)}, u32[]{:S(2)}) %all-to-all-start.2) | async-done | bytes 2359328 | tf_op jit(solution)/shard_map/all_to_all | solution.py:79
  219.1 4.3 reshape.191
  223.5 4.6 %multiply_convert_fusion.1 = bf16[576,768]{1,0:T(8,128)(2,1)S(1)} fusion(f32[576,768]{1,0:T(8,128)} %fusion.7, bf16[576,2048]{1,0:T(8,128)(2,1)} %reshape.191, bf16[1,768,2048]{2,1,0:T(8,128)(2,1)S(1)} %copy-done), kind=kOutput, calls=%fused_computation.22 | convolution fusion | flops 1815920640 | bytes 8159232 | tf_op jit(solution)/shard_map/dot_general | solution.py:13
  233.1 4.9 %fusion.12 = bf16[576,2048]{1,0:T(8,128)(2,1)} fusion(bf16[1,768,2048]{2,1,0:T(8,128)(2,1)S(1)} %copy-done, f32[576,768]{1,0:T(8,128)} %fusion.7), kind=kOutput, calls=%fused_computation.20 | convolution fusion | flops 1815330816 | bytes 7274496 | tf_op jit(solution)/shard_map/dot_general | solution.py:21
  242.2 7.7 %all-to-all-start.1 = ((bf16[32,18,2048]{2,1,0:T(8,128)(2,1)}), bf16[32,18,2048]{2,1,0:T(8,128)(2,1)S(1)}, u32[]{:S(2)}, u32[]{:S(2)}) async-start(bf16[32,18,2048]{2,1,0:T(8,128)(2,1)} %reshape.188), calls=%async_computation.1 | async-start | bytes 6291456 | tf_op jit(solution)/shard_map/all_to_all | solution.py:66
  249.9 6.8 %fusion.9 = bf16[576,2048]{1,0:T(8,128)(2,1)} fusion(bf16[576,768]{1,0:T(8,128)(2,1)} %copy-done.7, bf16[1,2048,768]{2,1,0:T(8,128)(2,1)} %param.11), kind=kOutput, calls=%fused_computation.19 | convolution fusion | flops 1813118976 | bytes 6389760 | tf_op jit(solution)/shard_map/dot_general | solution.py:13
  256.7 4.3 reshape.192
  261.0 60.8 %all-to-all-done.1 = bf16[32,18,2048]{2,1,0:T(8,128)(2,1)S(1)} async-done(((bf16[32,18,2048]{2,1,0:T(8,128)(2,1)}), bf16[32,18,2048]{2,1,0:T(8,128)(2,1)S(1)}, u32[]{:S(2)}, u32[]{:S(2)}) %all-to-all-start.1) | async-done | bytes 2359328 | tf_op jit(solution)/shard_map/all_to_all | solution.py:66
  323.5 5.6 %all-to-all-start.3 = ((bf16[32,18,2048]{2,1,0:T(8,128)(2,1)}), bf16[32,18,2048]{2,1,0:T(8,128)(2,1)}, u32[]{:S(2)}, u32[]{:S(2)}) async-start(bf16[32,18,2048]{2,1,0:T(8,128)(2,1)} %reshape.192), calls=%async_computation.3 | async-start | bytes 6291456 | tf_op jit(solution)/shard_map/all_to_all | solution.py:84
  329.4 6.6 %fusion.15 = bf16[1,768,2048]{2,1,0:T(8,128)(2,1)} fusion(bf16[576,2048]{1,0:T(8,128)(2,1)} %reshape.191, f32[576,768]{1,0:T(8,128)} %fusion.7), kind=kOutput, calls=%fused_computation.21 | convolution fusion | flops 1815724032 | bytes 7274496 | tf_op jit(solution)/shard_map/dot_general | solution.py:13
  342.2 58.1 %all-to-all-done.3 = bf16[32,18,2048]{2,1,0:T(8,128)(2,1)} async-done(((bf16[32,18,2048]{2,1,0:T(8,128)(2,1)}), bf16[32,18,2048]{2,1,0:T(8,128)(2,1)}, u32[]{:S(2)}, u32[]{:S(2)}) %all-to-all-start.3) | async-done | bytes 2359328 | tf_op jit(solution)/shard_map/all_to_all | solution.py:84
  411.8 15.6 %reduce_sum.55 = bf16[2048,768]{1,0:T(8,128)(2,1)} reduce(bf16[8,2048,768]{2,1,0:T(8,128)(2,1)} %bitcast.95, bf16[]{:T(256)} %constant.96.clone.1), dimensions={0}, to_apply=%region_7.8 | reduce | flops 11010048 | bytes 28311554 | tf_op jit(solution)/shard_map/reduce_sum | solution.py:96
  427.4 6.4 %all-reduce.2.cloned.1.call-done = bf16[1,768,2048]{2,1,0:T(8,128)(2,1)} async-done(((bf16[1,768,2048]{2,1,0:T(8,128)(2,1)}), bf16[1,768,2048]{2,1,0:T(8,128)(2,1)}) %all-reduce.2.cloned.1.call-update) | async-done | bytes 3145744 | tf_op jit(solution)/shard_map/psum | solution.py:97
  (52 shorter events, 39.0 us)
Async XLA Ops:
  7.2 216.3 %copy-start = (bf16[1,768,2048]{2,1,0:T(8,128)(2,1)S(1)}, bf16[1,768,2048]{2,1,0:T(8,128)(2,1)}, u32[]{:S(2)}) copy-start(bf16[1,768,2048]{2,1,0:T(8,128)(2,1)} %param.12) | copy-start | bytes 9437188
  57.5 12.4 %copy-start.6 = (f32[48,8]{0,1:T(8,128)S(1)}, f32[48,8]{0,1:T(8,128)}, u32[]{:S(2)}) copy-start(f32[48,8]{0,1:T(8,128)} %param.10) | copy-start | bytes 4612
  57.5 12.6 %copy-start.5 = (bf16[48,2048]{1,0:T(8,128)(2,1)S(1)}, bf16[48,2048]{1,0:T(8,128)(2,1)}, u32[]{:S(2)}) copy-start(bf16[48,2048]{1,0:T(8,128)(2,1)} %param.13) | copy-start | bytes 589828
  57.5 83.6 %all-to-all-start = ((bf16[32,18,2048]{2,1,0:T(8,128)(2,1)}), bf16[32,18,2048]{2,1,0:T(8,128)(2,1)}, u32[]{:S(2)}, u32[]{:S(2)}) async-start(bf16[32,18,2048]{2,1,0:T(8,128)(2,1)} %reshape.186), calls=%async_computation | async-start | bytes 6291456 | tf_op jit(solution)/shard_map/all_to_all | solution.py:61
  141.0 78.1 %all-to-all-start.2 = ((bf16[32,18,2048]{2,1,0:T(8,128)(2,1)}), bf16[32,18,2048]{2,1,0:T(8,128)(2,1)}, u32[]{:S(2)}, u32[]{:S(2)}) async-start(bf16[32,18,2048]{2,1,0:T(8,128)(2,1)} %reshape.190), calls=%async_computation.2 | async-start | bytes 6291456 | tf_op jit(solution)/shard_map/all_to_all | solution.py:79
  148.4 263.4 %all-gather.3.cloned.1.call-start = ((), (), s32[]{:S(2)}) async-start(), calls=%async_computation.5 | async-start | bytes 28311552 | tf_op jit(solution)/shard_map/all_gather | solution.py:96
  223.5 5.6 %copy-start.4 = (bf16[576,2048]{1,0:T(8,128)(2,1)S(1)}, bf16[576,2048]{1,0:T(8,128)(2,1)}, u32[]{:S(2)}) copy-start(bf16[576,2048]{1,0:T(8,128)(2,1)} %reshape.187) | copy-start | bytes 7077892
  228.1 0.9 copy-start.7
  242.2 79.6 %all-to-all-start.1 = ((bf16[32,18,2048]{2,1,0:T(8,128)(2,1)}), bf16[32,18,2048]{2,1,0:T(8,128)(2,1)S(1)}, u32[]{:S(2)}, u32[]{:S(2)}) async-start(bf16[32,18,2048]{2,1,0:T(8,128)(2,1)} %reshape.188), calls=%async_computation.1 | async-start | bytes 6291456 | tf_op jit(solution)/shard_map/all_to_all | solution.py:66
  321.8 1.7 copy-start.2
  323.5 76.8 %all-to-all-start.3 = ((bf16[32,18,2048]{2,1,0:T(8,128)(2,1)}), bf16[32,18,2048]{2,1,0:T(8,128)(2,1)}, u32[]{:S(2)}, u32[]{:S(2)}) async-start(bf16[32,18,2048]{2,1,0:T(8,128)(2,1)} %reshape.192), calls=%async_computation.3 | async-start | bytes 6291456 | tf_op jit(solution)/shard_map/all_to_all | solution.py:84
  329.1 104.7 %all-reduce.2.cloned.1.call-start = ((), (), s32[]{:S(2)}) async-start(), calls=%async_computation.4 | async-start | bytes 6291456 | tf_op jit(solution)/shard_map/psum | solution.py:97
  406.4 3.3 copy-start.3
  433.8 4.1 copy-start.1
Sparse Core Ops, SparseCore 0:
  233.2 121.8 all-gather.2
  357.4 76.2 all-reduce.1
